TPU v7x, 32 devices: a whole 2x2x4 slice. The times are simulated.
32 devices in a mesh: row: 8 (over z, y), col: 4 (over x, core).
Axes of the slice: x: 2, y: 2, z: 4, core: 2. Of those that a mesh axis runs over, the one named last changes fastest.
Arguments:
- trailing: float32 [8192, 4096], P('row', 'col'), may hold values from -6 to 6
- panel_y: float32 [8192, 256], P(('row', 'col')), may hold values from -0.1875 to 0.1875
- panel_t: float32 [2048, 256], P('row'), may hold values from 0.5 to 1.5
- tree_v: float32 [3, 2048, 256], P(None, 'row'), may hold values from -0.375 to 0.375, as said below
- tree_t: float32 [3, 2048, 256], P(None, 'row'), may hold values from 0.5 to 1.5, as said below
Outputs:
- updated: float32 [8192, 4096], P('row', 'col')
Inputs may be any that keep to these rules, and one draw needn't show every extreme that they name: For each level l, the blocks of 256 rows that tree_v[l] holds for two tile rows that differ only in bit l are equal. For each level l, the blocks of 256 rows that tree_t[l] holds for two tile rows that differ only in bit l are equal.
All inputs are finite; a program needn't handle non-finite values.
Results may differ from a plain program's by a relative error of at most 0.0001.
Values sent between devices are 32-bit elements; how exact they have to be, the bound alone decides.
A program may use at most 64 MiB of HBM per device.

v0:
```python
import math

import jax
import jax.numpy as jnp
from jax import lax
from jax.sharding import PartitionSpec as P


def from_partner(block, axis, bit):
    count = lax.axis_size(axis)
    route = []
    for low in range(count):
        high = low | 1 << bit
        if high != low and high < count:
            route += [(low, high), (high, low)]
    return lax.ppermute(block, axis, route)


def unit_lower(values):
    rows = jnp.arange(values.shape[0])[:, None]
    cols = jnp.arange(values.shape[1])[None, :]
    return jnp.where(
        rows > cols, values, jnp.where(rows == cols, jnp.float32(1.0), jnp.float32(0.0))
    )


def triangle_factor(values):
    width = values.shape[-1]
    rows = jnp.arange(width)[:, None]
    cols = jnp.arange(width)[None, :]
    scale = 2.0 / math.sqrt(width)
    return jnp.where(
        rows == cols, values, jnp.where(cols > rows, (values - 1.0) * scale, jnp.float32(0.0))
    )


def upper_part(values):
    width = values.shape[-1]
    rows = jnp.arange(width)[:, None]
    cols = jnp.arange(width)[None, :]
    return jnp.where(cols >= rows, values, jnp.float32(0.0))


def pair_update(first, second, vees, tees):
    highest = lax.Precision.HIGHEST
    summed = first + jnp.einsum("kb,kn->bn", vees, second, precision=highest)
    factor = jnp.einsum("kb,kn->bn", tees, summed, precision=highest)
    return (first - factor, second - jnp.dot(vees, factor, precision=highest))


def per_device(trailing, panel_y, panel_t, tree_v, tree_t):
    highest = lax.Precision.HIGHEST
    width = panel_t.shape[1]
    gathered = lax.all_gather(panel_y, "col", axis=0, tiled=True)
    lower = unit_lower(gathered)
    proj = jnp.einsum("mb,mn->bn", lower, trailing, precision=highest)
    weight = jnp.einsum("kb,kn->bn", triangle_factor(panel_t), proj, precision=highest)
    local = trailing - jnp.dot(lower, weight, precision=highest)
    top = local[:width]
    rest = local[width:]
    position = lax.axis_index("row")
    for level in range(tree_v.shape[0]):
        leader = position >> level & 1 == 0
        vees = upper_part(tree_v[level])
        tees = triangle_factor(tree_t[level])
        other = from_partner(top, "row", level)
        first = jnp.where(leader, top, other)
        second = jnp.where(leader, other, top)
        new_first, new_second = pair_update(first, second, vees, tees)
        top = jnp.where(leader, new_first, new_second)
    return jnp.concatenate([top, rest], axis=0)


def solution(mesh):
    placed = (
        P("row", "col"),
        P(("row", "col"), None),
        P("row", None),
        P(None, "row", None),
        P(None, "row", None),
    )
    return jax.shard_map(
        per_device, mesh=mesh, in_specs=placed, out_specs=P("row", "col"), check_vma=False
    )
```

profile of v0, /device:TPU:0, one launch (start us, length us, event | category | flops | bytes accessed | tf_op | source)
XLA Modules:
  0.0 164.8 jit_solution(18364311982936171738)
XLA Ops:
  6.5 0.0 copy-start.6
  6.5 0.0 all-gather.2.cloned.1.call-start
  6.5 0.7 all-gather.2.cloned.1.call-update
  7.3 21.1 %all-gather.2.cloned.1.call-done = f32[1024,256]{1,0:T(8,128)} async-done(((f32[256,256]{1,0:T(8,128)}), f32[1024,256]{1,0:T(8,128)}) %all-gather.2.cloned.1.call-update) | async-done | bytes 1048592 | tf_op jit(solution)/shard_map/all_gather | solution.py:54
  28.4 0.0 copy-start.2
  28.4 0.0 copy-start.3
  28.4 6.0 %fusion = f32[256,1024]{1,0:T(8,128)S(1)} fusion(f32[1024,1024]{1,0:T(8,128)} %param.5, f32[1024,256]{1,0:T(8,128)} %all-gather.2.cloned.1.call-done), kind=kOutput, calls=%fused_computation.14 | convolution fusion | flops 3222274048 | bytes 6291456 | tf_op jit(solution)/shard_map/mb,mn->bn/dot_general | solution.py:56
  34.4 0.0 copy-done.6
  34.4 1.1 fusion.17
  35.5 0.0 copy-done.2
  35.5 0.0 copy-done.3
  35.5 0.0 copy-start.4
  35.5 3.7 %convolution_subtract_fusion = f32[1024,1024]{1,0:T(8,128)S(1)} fusion(f32[1024,1024]{1,0:T(8,128)S(1)} %copy-done.2, f32[256,1024]{1,0:T(8,128)S(1)} %fusion.17, f32[1024,256]{1,0:T(8,128)S(1)} %copy-done.3), kind=kOutput, calls=%fused_computation.1 | convolution fusion | flops 3223322624 | bytes 10485760 | tf_op jit(solution)/shard_map/dot_general | solution.py:58
  39.2 0.0 copy-start
  39.3 2.0 %copy-done = f32[1024,1024]{1,0:T(8,128)} copy-done((f32[1024,1024]{1,0:T(8,128)}, f32[1024,1024]{1,0:T(8,128)S(1)}, u32[]{:S(2)}) %copy-start) | copy-done | bytes 4194328
  41.3 0.1 slice.32
  41.3 1.5 collective-permute-start
  42.9 0.0 copy-start.1
  42.9 23.8 %collective-permute-done = f32[256,1024]{1,0:T(8,128)S(1)} collective-permute-done((f32[256,1024]{1,0:T(8,128)S(1)}, f32[256,1024]{1,0:T(8,128)S(1)}, u32[]{:S(2)}, u32[]{:S(2)}) %collective-permute-start) | collective-permute-done | bytes 1048608 | tf_op jit(solution)/shard_map/ppermute | solution.py:16
  66.7 0.0 copy-done.4
  66.7 2.7 %convolution_add_fusion.2 = f32[256,1024]{1,0:T(8,128)S(1)} fusion(f32[256,1024]{1,0:T(8,128)S(1)} %collective-permute-done, pred[]{:T(512)S(6)} %eq.100, f32[3,256,256]{2,1,0:T(8,128)S(1)} %copy-done.4, f32[1024,1024]{1,0:T(8,128)} %copy-done), kind=kOutput, calls=%fused_computation.7 | convolution fusion | flops 806223872 | bytes 5506048 | tf_op jit(solution)/shard_map/kb,kn->bn/dot_general | solution.py:46
  69.4 2.0 %fusion.13 = f32[256,1024]{1,0:T(8,128)S(1)} fusion(f32[256,1024]{1,0:T(8,128)S(1)} %convolution_add_fusion.2, f32[3,256,256]{2,1,0:T(8,128)} %param.9), kind=kOutput, calls=%fused_computation.42 | convolution fusion | flops 805699584 | bytes 2359296 | tf_op jit(solution)/shard_map/kb,kn->bn/dot_general | solution.py:47
  71.4 0.0 copy-done.1
  71.4 1.3 subtract_select_fusion.2
  72.7 1.5 collective-permute-start.1
  74.2 23.0 %collective-permute-done.1 = f32[256,1024]{1,0:T(8,128)S(1)} collective-permute-done((f32[256,1024]{1,0:T(8,128)S(1)}, f32[256,1024]{1,0:T(8,128)S(1)}, u32[]{:S(2)}, u32[]{:S(2)}) %collective-permute-start.1) | collective-permute-done | bytes 1048608 | tf_op jit(solution)/shard_map/ppermute | solution.py:16
  97.3 2.1 %convolution_add_fusion.1 = f32[256,1024]{1,0:T(8,128)S(1)} fusion(f32[256,1024]{1,0:T(8,128)S(1)} %subtract_select_fusion.2, f32[256,1024]{1,0:T(8,128)S(1)} %collective-permute-done.1, pred[]{:T(512)S(6)} %eq.99, f32[3,256,256]{2,1,0:T(8,128)} %param.8), kind=kOutput, calls=%fused_computation.5 | convolution fusion | flops 806223872 | bytes 5506048 | tf_op jit(solution)/shard_map/kb,kn->bn/dot_general | solution.py:46
  99.3 2.0 %fusion.10 = f32[256,1024]{1,0:T(8,128)S(1)} fusion(f32[256,1024]{1,0:T(8,128)S(1)} %convolution_add_fusion.1, f32[3,256,256]{2,1,0:T(8,128)} %param.9), kind=kOutput, calls=%fused_computation.36 | convolution fusion | flops 805699584 | bytes 2359296 | tf_op jit(solution)/shard_map/kb,kn->bn/dot_general | solution.py:47
  101.3 2.2 %subtract_select_fusion.1 = f32[256,1024]{1,0:T(8,128)S(1)} fusion(f32[256,1024]{1,0:T(8,128)S(1)} %fusion.10, pred[]{:T(512)S(6)} %eq.99, f32[256,1024]{1,0:T(8,128)S(1)} %subtract_select_fusion.2, f32[256,1024]{1,0:T(8,128)S(1)} %collective-permute-done.1, f32[3,256,256]{2,1,0:T(8,128)} %param.8), kind=kOutput, calls=%fused_computation.9 | convolution fusion | flops 806748160 | bytes 5505025 | tf_op jit(solution)/shard_map/dot_general | solution.py:48
  103.5 0.0 copy-start.5
  103.6 2.5 %collective-permute-start.2 = (f32[256,1024]{1,0:T(8,128)S(1)}, f32[256,1024]{1,0:T(8,128)S(1)}, u32[]{:S(2)}, u32[]{:S(2)}) collective-permute-start(f32[256,1024]{1,0:T(8,128)S(1)} %subtract_select_fusion.1), channel_id=1, source_target_pairs={{0,16},{16,0},{4,20},{20,4},{8,24},{24,8},{12,28},{28,12},{1,17},{... | collective-permute-start | bytes 3145736 | tf_op jit(solution)/shard_map/ppermute | solution.py:16
  106.0 44.5 %collective-permute-done.2 = f32[256,1024]{1,0:T(8,128)S(1)} collective-permute-done((f32[256,1024]{1,0:T(8,128)S(1)}, f32[256,1024]{1,0:T(8,128)S(1)}, u32[]{:S(2)}, u32[]{:S(2)}) %collective-permute-start.2) | collective-permute-done | bytes 1048608 | tf_op jit(solution)/shard_map/ppermute | solution.py:16
  150.6 0.0 copy-done.5
  150.6 1.3 convolution_add_fusion
  151.9 0.0 slice-start
  151.9 2.2 %fusion.7 = f32[256,1024]{1,0:T(8,128)S(1)} fusion(f32[256,1024]{1,0:T(8,128)S(1)} %convolution_add_fusion, f32[3,256,256]{2,1,0:T(8,128)} %param.9), kind=kOutput, calls=%fused_computation.30 | convolution fusion | flops 805699584 | bytes 2359296 | tf_op jit(solution)/shard_map/kb,kn->bn/dot_general | solution.py:47
  154.0 1.3 subtract_select_fusion
  155.3 0.0 slice-done
  155.3 2.6 %pad_maximum_fusion = f32[1024,1024]{1,0:T(8,128)} fusion(f32[768,1024]{1,0:T(8,128)S(1)} %slice-done, f32[256,1024]{1,0:T(8,128)S(1)} %subtract_select_fusion), kind=kLoop, calls=%fused_computation | loop fusion | flops 1048576 | bytes 8388608 | tf_op jit(solution)/shard_map/concatenate | solution.py:71
Async XLA Ops:
  6.5 27.9 %copy-start.6 = (f32[256,256]{1,0:T(8,128)S(1)}, f32[256,256]{1,0:T(8,128)}, u32[]{:S(2)}) copy-start(f32[256,256]{1,0:T(8,128)} %param.7) | copy-start | bytes 786436
  6.5 21.8 %all-gather.2.cloned.1.call-start = ((), (), s32[]{:S(2)}) async-start(), calls=%async_computation | async-start | bytes 1310720 | tf_op jit(solution)/shard_map/all_gather | solution.py:54
  28.4 7.1 %copy-start.2 = (f32[1024,1024]{1,0:T(8,128)S(1)}, f32[1024,1024]{1,0:T(8,128)}, u32[]{:S(2)}) copy-start(f32[1024,1024]{1,0:T(8,128)} %param.5) | copy-start | bytes 12582916
  28.4 7.1 %copy-start.3 = (f32[1024,256]{1,0:T(8,128)S(1)}, f32[1024,256]{1,0:T(8,128)}, u32[]{:S(2)}) copy-start(f32[1024,256]{1,0:T(8,128)} %all-gather.2.cloned.1.call-done) | copy-start | bytes 3145732
  35.5 31.2 %copy-start.4 = (f32[3,256,256]{2,1,0:T(8,128)S(1)}, f32[3,256,256]{2,1,0:T(8,128)}, u32[]{:S(2)}) copy-start(f32[3,256,256]{2,1,0:T(8,128)} %param.8) | copy-start | bytes 2359300
  39.2 2.0 %copy-start = (f32[1024,1024]{1,0:T(8,128)}, f32[1024,1024]{1,0:T(8,128)S(1)}, u32[]{:S(2)}) copy-start(f32[1024,1024]{1,0:T(8,128)S(1)} %convolution_subtract_fusion) | copy-start | bytes 12582916
  41.3 25.4 %collective-permute-start = (f32[256,1024]{1,0:T(8,128)S(1)}, f32[256,1024]{1,0:T(8,128)S(1)}, u32[]{:S(2)}, u32[]{:S(2)}) collective-permute-start(f32[256,1024]{1,0:T(8,128)S(1)} %slice.32), channel_id=1, source_target_pairs={{0,4},{4,0},{8,12},{12,8},{16,20},{20,16},{24,28},{28,24},{1,5},{5... | collective-permute-start | bytes 3145736 | tf_op jit(solution)/shard_map/ppermute | solution.py:16
  42.9 28.5 %copy-start.1 = (f32[1024,1024]{1,0:T(8,128)S(1)}, f32[1024,1024]{1,0:T(8,128)}, u32[]{:S(2)}) copy-start(f32[1024,1024]{1,0:T(8,128)} %copy-done) | copy-start | bytes 12582916
  72.7 24.6 %collective-permute-start.1 = (f32[256,1024]{1,0:T(8,128)S(1)}, f32[256,1024]{1,0:T(8,128)S(1)}, u32[]{:S(2)}, u32[]{:S(2)}) collective-permute-start(f32[256,1024]{1,0:T(8,128)S(1)} %subtract_select_fusion.2), channel_id=1, source_target_pairs={{0,8},{8,0},{4,12},{12,4},{16,24},{24,16},{20,28},{28,20},{1,9},{9... | collective-permute-start | bytes 3145736 | tf_op jit(solution)/shard_map/ppermute | solution.py:16
  103.5 47.0 %copy-start.5 = (f32[3,256,256]{2,1,0:T(8,128)S(1)}, f32[3,256,256]{2,1,0:T(8,128)}, u32[]{:S(2)}) copy-start(f32[3,256,256]{2,1,0:T(8,128)} %param.8) | copy-start | bytes 2359300
  103.6 47.0 %collective-permute-start.2 = (f32[256,1024]{1,0:T(8,128)S(1)}, f32[256,1024]{1,0:T(8,128)S(1)}, u32[]{:S(2)}, u32[]{:S(2)}) collective-permute-start(f32[256,1024]{1,0:T(8,128)S(1)} %subtract_select_fusion.1), channel_id=1, source_target_pairs={{0,16},{16,0},{4,20},{20,4},{8,24},{24,8},{12,28},{28,12},{1,17},{... | collective-permute-start | bytes 3145736 | tf_op jit(solution)/shard_map/ppermute | solution.py:16
  151.9 3.4 %slice-start = ((f32[1024,1024]{1,0:T(8,128)}), f32[768,1024]{1,0:T(8,128)S(1)}, s32[]{:S(2)}) async-start(f32[1024,1024]{1,0:T(8,128)} %copy-done), calls=%async_computation.1 | async-start | bytes 6291456 | tf_op jit(solution)/shard_map/slice | solution.py:60
Sparse Core Ops, SparseCore 0:
  8.9 19.4 all-gather.1
where the time goes:
time: 165 us
  waiting for transfers between devices  113 us (68%)
  matrix products  27.7 us (17%)
  between operations  13.6 us (8%)
  starting transfers between devices  5.55 us (3%)
  other arithmetic  2.6 us (2%)
  local copies, waits for them, and re-layouts  2.11 us (1%)
    ppermute x3, waiting for transfers between devices, from_partner(): return lax.ppermute(block, axis, route)  91.4 us
    all_gather x1, waiting for transfers between devices, per_device(): gathered = lax.all_gather(panel_y, 'col', axis=0, tiled=True)  21.1 us
    dot_general x3, matrix products, pair_update(): factor = jnp.einsum('kb,kn->bn', tees, summed, precision=highest)  6.16 us
    dot_general x1, matrix products, per_device(): proj = jnp.einsum('mb,mn->bn', lower, trailing, precision=highest)  6.04 us
    dot_general x3, matrix products, pair_update(): summed = first + jnp.einsum('kb,kn->bn', vees, second, precision=highest)  6.03 us
    ppermute x3, starting transfers between devices, from_partner(): return lax.ppermute(block, axis, route)  5.55 us
    dot_general x3, matrix products, pair_update(): return (first - factor, second - jnp.dot(vees, factor, precision=highest))  4.75 us
    dot_general x1, matrix products, per_device(): local = trailing - jnp.dot(lower, weight, precision=highest)  3.72 us
  transfers between devices with their start and end apart: 4, of which 4 were waited for; matrix products, arithmetic and copies ran while one was open for 0% of the time, Pallas kernels for 0%

commit v1 on v0

v1 whole, which is shorter than its diff:
```python
import functools
import math

import jax
import jax.numpy as jnp
from jax import lax
from jax.experimental import pallas as pl
from jax.experimental.pallas import tpu as pltpu
from jax.sharding import PartitionSpec as P

CHUNK = 128
MESH = pl.DeviceIdType.MESH


def split(x):
    high = x.astype(jnp.bfloat16)
    low = (x - high.astype(jnp.float32)).astype(jnp.bfloat16)
    return high, low


def dot3(lhs_high, lhs_low, rhs):
    high, low = split(rhs)
    dot = functools.partial(jnp.dot, preferred_element_type=jnp.float32)
    return dot(lhs_high, high) + (dot(lhs_high, low) + dot(lhs_low, high))


def grid_of(shape, row_offset=0):
    rows = lax.broadcasted_iota(jnp.int32, shape, 0) + row_offset
    cols = lax.broadcasted_iota(jnp.int32, shape, 1)
    return rows, cols


def triangle_factor(values):
    width = values.shape[-1]
    rows, cols = grid_of(values.shape)
    scale = 2.0 / math.sqrt(width)
    return jnp.where(
        rows == cols, values, jnp.where(cols > rows, (values - 1.0) * scale, jnp.float32(0.0))
    )


def kernel(
    n_col, levels, chunks, width, depth,
    c_hbm, y_hbm, t_hbm, v_hbm, tt_hbm, out_hbm,
    c_v, y_v, t_v, v_v, tt_v, w_v, z_v, r_v,
    yt_s, yb_s, t_s, at_s, b_s,
    c_sem, in_sem, out_sem, ys_sem, yr_sem, s_sem, r_sem,
):
    row = lax.axis_index("row")
    col = lax.axis_index("col")
    chunk = c_v.shape[2]
    rest = c_v.shape[1] - width
    bits = [1 << b for b in range(n_col.bit_length() - 2, -1, -1)]

    def columns(k):
        return pl.ds(pl.multiple_of(k * chunk, chunk), chunk)

    def load_c(k):
        return pltpu.make_async_copy(c_hbm.at[:, columns(k)], c_v.at[k], c_sem.at[k])

    own_y = pltpu.make_async_copy(y_hbm, y_v.at[col], in_sem.at[0])
    load_t = pltpu.make_async_copy(t_hbm, t_v, in_sem.at[1])
    load_v = pltpu.make_async_copy(v_hbm, v_v, in_sem.at[2])
    load_tt = pltpu.make_async_copy(tt_hbm, tt_v, in_sem.at[3])
    own_y.start()

    barrier = pltpu.get_barrier_semaphore()
    partners = [(row, col ^ bit) for bit in bits]
    partners += [(row ^ (1 << level), col) for level in range(levels)]
    for partner in partners:
        pl.semaphore_signal(barrier, inc=1, device_id=partner, device_id_type=MESH)
    load_v.start()
    load_tt.start()
    load_t.start()
    for k in range(chunks):
        load_c(k).start()
    own_y.wait()
    pl.semaphore_wait(barrier, len(partners))

    def send_y(off, bit):
        block = col ^ off
        return pltpu.make_async_remote_copy(
            src_ref=y_v.at[block],
            dst_ref=y_v.at[block],
            send_sem=ys_sem.at[off | bit],
            recv_sem=yr_sem.at[off | bit],
            device_id=(row, col ^ bit),
            device_id_type=MESH,
        )

    def arrived_y(off):
        return pltpu.make_async_remote_copy(
            src_ref=y_v.at[col ^ off],
            dst_ref=y_v.at[col ^ off],
            send_sem=ys_sem.at[off],
            recv_sem=yr_sem.at[off],
            device_id=(row, col ^ 1),
            device_id_type=MESH,
        )

    for bit in bits:
        send_y(0, bit).start()

    load_v.wait()
    load_tt.wait()
    load_t.wait()
    high, low = split(triangle_factor(t_v[...]).T)
    t_s[0], t_s[1] = high, low
    for level in range(levels):
        leader = (row >> level) & 1 == 0
        rows, cols = grid_of((width, width))
        vees = jnp.where(cols >= rows, v_v[level], jnp.float32(0.0))
        at_s[level, 0], at_s[level, 1] = split(vees.T)
        tees = triangle_factor(tt_v[level]).T
        vees_high, vees_low = split(vees)
        both = jnp.where(leader, tees, dot3(vees_high, vees_low, tees))
        b_s[level, 0], b_s[level, 1] = split(both)

    def take_y(off):
        block = col ^ off
        rows, cols = grid_of((depth, width), block * depth)
        lower = jnp.where(
            rows > cols,
            y_v[block],
            jnp.where(rows == cols, jnp.float32(1.0), jnp.float32(0.0)),
        )
        place = pl.ds(pl.multiple_of(block * depth, depth), depth)
        high, low = split(lower)
        yb_s[0, place, :] = high
        yb_s[1, place, :] = low
        high, low = split(lower.T)
        yt_s[0, :, place] = high
        yt_s[1, :, place] = low

    take_y(0)
    order = sorted(range(1, n_col), key=lambda off: (bin(off).count("1"), off))
    for off in order:
        arrived_y(off).wait_recv()
        for bit in bits:
            if bit < off & -off:
                send_y(off, bit).start()
        take_y(off)

    def exchange(level, k):
        return pltpu.make_async_remote_copy(
            src_ref=z_v.at[level, k],
            dst_ref=r_v.at[level, k],
            send_sem=s_sem.at[level, k],
            recv_sem=r_sem.at[level, k],
            device_id=(row ^ (1 << level), col),
            device_id_type=MESH,
        )

    def give(level, k, top):
        leader = (row >> level) & 1 == 0
        down = dot3(at_s[level, 0], at_s[level, 1], top)
        z_v[level, k] = jnp.where(leader, top, down)
        exchange(level, k).start()

    def local(k):
        load_c(k).wait()
        proj = dot3(yt_s[0], yt_s[1], c_v[k])
        weight = dot3(t_s[0], t_s[1], proj)
        w_v[k] = weight
        top = c_v[k, :width, :] - dot3(yb_s[0, :width, :], yb_s[1, :width, :], weight)
        c_v[k, :width, :] = top
        give(0, k, top)

    def combine(level, k):
        exchange(level, k).wait_recv()
        total = z_v[level, k] + r_v[level, k]
        top = c_v[k, :width, :] - dot3(b_s[level, 0], b_s[level, 1], total)
        c_v[k, :width, :] = top
        return top

    def store_top(k):
        return pltpu.make_async_copy(
            c_v.at[k, pl.ds(0, width), :], out_hbm.at[pl.ds(0, width), columns(k)], out_sem.at[0, k]
        )

    def store_rest(k):
        return pltpu.make_async_copy(
            c_v.at[k, pl.ds(width, rest), :],
            out_hbm.at[pl.ds(width, rest), columns(k)],
            out_sem.at[1, k],
        )

    def step(t, carry):
        @pl.when(t < chunks)
        def _():
            local(t)

        for level in range(levels - 1):
            k = t - 1 - level

            @pl.when((k >= 0) & (k < chunks))
            def _():
                top = combine(level, k)
                give(level + 1, k, top)

        return carry

    lax.fori_loop(0, chunks + levels - 1, step, 0)

    def finish(k, carry):
        c_v[k, width:, :] = c_v[k, width:, :] - dot3(
            yb_s[0, width:, :], yb_s[1, width:, :], w_v[k]
        )
        store_rest(k).start()
        combine(levels - 1, k)
        store_top(k).start()
        return carry

    lax.fori_loop(0, chunks, finish, 0)

    for bit in bits:
        for off in range(0, n_col, 2 * bit):
            send_y(off, bit).wait_send()

    def drain(k, carry):
        for level in range(levels):
            exchange(level, k).wait_send()
        store_top(k).wait()
        store_rest(k).wait()
        return carry

    lax.fori_loop(0, chunks, drain, 0)


def per_device(trailing, panel_y, panel_t, tree_v, tree_t):
    n_col = lax.axis_size("col")
    depth, width = panel_y.shape
    height, extent = trailing.shape
    levels = tree_v.shape[0]
    chunk = min(CHUNK, extent)
    chunks = extent // chunk
    f32, bf16 = jnp.float32, jnp.bfloat16
    products = height * width * 2 + width * width * (1 + 2 * levels)
    return pl.pallas_call(
        functools.partial(kernel, n_col, levels, chunks, width, depth),
        out_shape=jax.ShapeDtypeStruct(trailing.shape, f32),
        in_specs=[pl.BlockSpec(memory_space=pltpu.HBM)] * 5,
        out_specs=pl.BlockSpec(memory_space=pl.ANY),
        scratch_shapes=[
            pltpu.VMEM((chunks, height, chunk), f32),
            pltpu.VMEM((n_col, depth, width), f32),
            pltpu.VMEM((width, width), f32),
            pltpu.VMEM((levels, width, width), f32),
            pltpu.VMEM((levels, width, width), f32),
            pltpu.VMEM((chunks, width, chunk), f32),
            pltpu.VMEM((levels, chunks, width, chunk), f32),
            pltpu.VMEM((levels, chunks, width, chunk), f32),
            pltpu.VMEM((2, width, height), bf16),
            pltpu.VMEM((2, height, width), bf16),
            pltpu.VMEM((2, width, width), bf16),
            pltpu.VMEM((levels, 2, width, width), bf16),
            pltpu.VMEM((levels, 2, width, width), bf16),
            pltpu.SemaphoreType.DMA((chunks,)),
            pltpu.SemaphoreType.DMA((4,)),
            pltpu.SemaphoreType.DMA((2, chunks)),
            pltpu.SemaphoreType.DMA((n_col,)),
            pltpu.SemaphoreType.DMA((n_col,)),
            pltpu.SemaphoreType.DMA((levels, chunks)),
            pltpu.SemaphoreType.DMA((levels, chunks)),
        ],
        compiler_params=pltpu.CompilerParams(
            collective_id=0, has_side_effects=True, vmem_limit_bytes=40 * 1024 * 1024
        ),
        cost_estimate=pl.CostEstimate(
            flops=6 * products * extent,
            bytes_accessed=8 * height * extent,
            transcendentals=0,
        ),
    )(trailing, panel_y, panel_t, tree_v, tree_t)


def solution(mesh):
    placed = (
        P("row", "col"),
        P(("row", "col"), None),
        P("row", None),
        P(None, "row", None),
        P(None, "row", None),
    )
    return jax.shard_map(
        per_device, mesh=mesh, in_specs=placed, out_specs=P("row", "col"), check_vma=False
    )
```

time: 165 us -> 82.8 us (0.50)
  waiting for transfers between devices: 113 us -> 0 us
  Pallas kernels: 0 us -> 74.1 us
  matrix products: 27.7 us -> 0 us
  between operations: 13.6 us -> 0.01 us
  local copies, waits for them, and re-layouts: 2.11 us -> 8.37 us
  starting transfers between devices: 5.55 us -> 0 us
  other arithmetic: 2.6 us -> 0 us
    ppermute x3 -> x0, waiting for transfers between devices: 91.4 us -> none  [from_partner(): return lax.ppermute(block, axis, route)]
    pallas_call x0 -> x1, Pallas kernels: none -> 74.1 us  [per_device(): pl.pallas_call(functools.partial(kernel, n_col, levels, chunks, width, de...]
    dot_general x12 -> x0, matrix products: 27.7 us -> none  [the longest x3 6.16 us: pair_update(): factor = jnp.einsum('kb,kn->bn', tees, summed, precision=highest)]
    all_gather x1 -> x0, waiting for transfers between devices: 21.1 us -> none  [per_device(): gathered = lax.all_gather(panel_y, 'col', axis=0, tiled=True)]
    unnamed x14 -> x11, local copies, waits for them, and re-layouts: 2.04 us -> 8.37 us
    ppermute x3 -> x0, starting transfers between devices: 5.55 us -> none  [from_partner(): return lax.ppermute(block, axis, route)]
    concatenate x1 -> x0, other arithmetic: 2.6 us -> none  [per_device(): return jnp.concatenate([top, rest], axis=0)]
  transfers between devices with their start and end apart: 4 -> 0, of which waited for: 4 -> 0; matrix products, arithmetic and copies ran while one was open for 0% -> 0% of each run, Pallas kernels for 0% -> 0%
where the time goes in v1:
time: 82.8 us; the launch traced here: 82.5 us
  Pallas kernels  74.1 us (89%)
  local copies, waits for them, and re-layouts  8.37 us (10%)
    pallas_call x1, Pallas kernels, per_device(): pl.pallas_call(functools.partial(kernel, n_col, levels, chunks, width, de...  74.1 us
    unnamed x11, local copies, waits for them, and re-layouts  8.37 us

profile of v1, /device:TPU:0, one launch (start us, length us, event | category | flops | bytes accessed | tf_op | source)
XLA Modules:
  0.0 82.5 jit_solution(8353427169996965601)
XLA Ops:
  0.0 0.0 copy-start
  0.0 2.2 %copy-done = f32[1024,1024]{1,0:T(8,128)S(1)} copy-done((f32[1024,1024]{1,0:T(8,128)S(1)}, f32[1024,1024]{1,0:T(8,128)}, u32[]{:S(2)}) %copy-start) | copy-done | bytes 4194328
  2.2 0.0 copy-start.1
  2.2 1.1 %copy-done.1 = f32[3,256,256]{2,1,0:T(8,128)S(1)} copy-done((f32[3,256,256]{2,1,0:T(8,128)S(1)}, f32[3,256,256]{2,1,0:T(8,128)}, u32[]{:S(2)}) %copy-start.1) | copy-done | bytes 786456
  3.3 0.0 copy-start.2
  3.3 1.1 %copy-done.2 = f32[3,256,256]{2,1,0:T(8,128)S(1)} copy-done((f32[3,256,256]{2,1,0:T(8,128)S(1)}, f32[3,256,256]{2,1,0:T(8,128)}, u32[]{:S(2)}) %copy-start.2) | copy-done | bytes 786456
  4.5 0.0 copy-start.3
  4.5 0.9 %copy-done.3 = f32[256,256]{1,0:T(8,128)S(1)} copy-done((f32[256,256]{1,0:T(8,128)S(1)}, f32[256,256]{1,0:T(8,128)}, u32[]{:S(2)}) %copy-start.3) | copy-done | bytes 262168
  5.4 0.0 copy-start.4
  5.4 0.9 %copy-done.4 = f32[256,256]{1,0:T(8,128)S(1)} copy-done((f32[256,256]{1,0:T(8,128)S(1)}, f32[256,256]{1,0:T(8,128)}, u32[]{:S(2)}) %copy-start.4) | copy-done | bytes 262168
  6.4 74.1 %shard_map.55 = f32[1024,1024]{1,0:T(8,128)S(1)} custom-call(f32[1024,1024]{1,0:T(8,128)S(1)} %copy-done, f32[256,256]{1,0:T(8,128)S(1)} %copy-done.3, f32[256,256]{1,0:T(8,128)S(1)} %copy-done.4, f32[3,256,256]{2,1,0:T(8,128)S(1)} %copy-done.1, f32[3,256,256]{2,1,0:T(8,128)S(1)} %copy-done.2), custom_call_target="tpu_custom_call" | custom-call | flops 6039797760 | bytes 8388608 | tf_op jit(solution)/shard_map/pallas_call | solution.py:239
  80.5 2.0 %copy.7 = f32[1024,1024]{1,0:T(8,128)} copy(f32[1024,1024]{1,0:T(8,128)S(1)} %shard_map.55) | data formatting | bytes 8388608
Async XLA Ops:
  0.0 2.2 %copy-start = (f32[1024,1024]{1,0:T(8,128)S(1)}, f32[1024,1024]{1,0:T(8,128)}, u32[]{:S(2)}) copy-start(f32[1024,1024]{1,0:T(8,128)} %c_hbm.1) | copy-start | bytes 12582916
  2.2 1.1 %copy-start.1 = (f32[3,256,256]{2,1,0:T(8,128)S(1)}, f32[3,256,256]{2,1,0:T(8,128)}, u32[]{:S(2)}) copy-start(f32[3,256,256]{2,1,0:T(8,128)} %v_hbm.1) | copy-start | bytes 2359300
  3.3 1.1 %copy-start.2 = (f32[3,256,256]{2,1,0:T(8,128)S(1)}, f32[3,256,256]{2,1,0:T(8,128)}, u32[]{:S(2)}) copy-start(f32[3,256,256]{2,1,0:T(8,128)} %tt_hbm.1) | copy-start | bytes 2359300
  4.5 0.9 %copy-start.3 = (f32[256,256]{1,0:T(8,128)S(1)}, f32[256,256]{1,0:T(8,128)}, u32[]{:S(2)}) copy-start(f32[256,256]{1,0:T(8,128)} %y_hbm.1) | copy-start | bytes 786436
  5.4 0.9 %copy-start.4 = (f32[256,256]{1,0:T(8,128)S(1)}, f32[256,256]{1,0:T(8,128)}, u32[]{:S(2)}) copy-start(f32[256,256]{1,0:T(8,128)} %t_hbm.1) | copy-start | bytes 786436

commit v2 on v1

v2 whole, which is shorter than its diff:
```python
import functools
import math

import jax
import jax.numpy as jnp
from jax import lax
from jax.experimental import pallas as pl
from jax.experimental.pallas import tpu as pltpu
from jax.sharding import PartitionSpec as P

CHUNK = 128
PARTS = 2
MESH = pl.DeviceIdType.MESH


def split(x):
    high = x.astype(jnp.bfloat16)
    low = (x - high.astype(jnp.float32)).astype(jnp.bfloat16)
    return high, low


def stack(x):
    return jnp.concatenate(split(x), axis=0)


def dot3(lhs, rhs):
    half = lhs.shape[0] // 2
    high, low = split(rhs)
    both = jnp.dot(lhs, high, preferred_element_type=jnp.float32)
    cross = jnp.dot(lhs[:half], low, preferred_element_type=jnp.float32)
    return both[:half] + (both[half:] + cross)


def grid_of(shape, row_offset=0):
    rows = lax.broadcasted_iota(jnp.int32, shape, 0) + row_offset
    cols = lax.broadcasted_iota(jnp.int32, shape, 1)
    return rows, cols


def triangle_factor(values):
    width = values.shape[-1]
    rows, cols = grid_of(values.shape)
    scale = 2.0 / math.sqrt(width)
    return jnp.where(
        rows == cols, values, jnp.where(cols > rows, (values - 1.0) * scale, jnp.float32(0.0))
    )


def kernel(
    n_col, levels, chunks, width, depth, parts,
    c_hbm, y_hbm, t_hbm, v_hbm, tt_hbm, out_hbm,
    c_v, y_v, t_v, v_v, tt_v, p_v, w_v, z_v, r_v,
    yr_s, t_s, a_s, b_s, f_s,
    c_sem, in_sem, out_sem, ys_sem, yr_sem, s_sem, r_sem,
):
    row = lax.axis_index("row")
    col = lax.axis_index("col")
    chunk = c_v.shape[2]
    rest = c_v.shape[1] - width
    pairs = chunks // 2
    share = depth // parts
    bits = [1 << b for b in range(n_col.bit_length() - 2, -1, -1)]

    def columns(k):
        return pl.ds(pl.multiple_of(k * chunk, chunk), chunk)

    def load_c(k):
        return pltpu.make_async_copy(c_hbm.at[:, columns(k)], c_v.at[k], c_sem.at[k])

    own_y = pltpu.make_async_copy(y_hbm, y_v.at[col], in_sem.at[0])
    load_t = pltpu.make_async_copy(t_hbm, t_v, in_sem.at[1])
    load_v = pltpu.make_async_copy(v_hbm, v_v, in_sem.at[2])
    load_tt = pltpu.make_async_copy(tt_hbm, tt_v, in_sem.at[3])
    own_y.start()

    barrier = pltpu.get_barrier_semaphore()
    partners = [(row, col ^ bit) for bit in bits]
    partners += [(row ^ (1 << level), col) for level in range(levels)]
    for partner in partners:
        pl.semaphore_signal(barrier, inc=1, device_id=partner, device_id_type=MESH)
    load_v.start()
    load_tt.start()
    load_t.start()
    for k in range(chunks):
        load_c(k).start()
    own_y.wait()
    pl.semaphore_wait(barrier, len(partners))

    def send_y(off, bit, part):
        place = y_v.at[col ^ off, pl.ds(part * share, share), :]
        return pltpu.make_async_remote_copy(
            src_ref=place,
            dst_ref=place,
            send_sem=ys_sem.at[part, off | bit],
            recv_sem=yr_sem.at[part, off | bit],
            device_id=(row, col ^ bit),
            device_id_type=MESH,
        )

    def arrived_y(off, part):
        place = y_v.at[col ^ off, pl.ds(part * share, share), :]
        return pltpu.make_async_remote_copy(
            src_ref=place,
            dst_ref=place,
            send_sem=ys_sem.at[part, off],
            recv_sem=yr_sem.at[part, off],
            device_id=(row, col ^ 1),
            device_id_type=MESH,
        )

    for bit in bits:
        for part in range(parts):
            send_y(0, bit, part).start()

    def pair_of(p, rows):
        return jnp.concatenate([c_v[2 * p, rows, :], c_v[2 * p + 1, rows, :]], axis=1)

    def leads(level):
        return (row >> level) & 1 == 0

    def prepare(level):
        rows, cols = grid_of((width, width))
        vees = jnp.where(cols >= rows, v_v[level], jnp.float32(0.0))
        a_s[level] = stack(vees.T)
        tees = triangle_factor(tt_v[level]).T
        both = jnp.where(leads(level), tees, dot3(stack(vees), tees))
        terms = split(both)
        if level == levels - 1:
            b_s[level, :width], b_s[level, 2 * width : 3 * width] = terms
        else:
            rows, cols = grid_of((width, width))
            after = jnp.where(cols >= rows, v_v[level + 1], jnp.float32(0.0)).T
            folded = split(jnp.where(leads(level + 1), both, dot3(stack(after), both)))
            for i in range(2):
                b_s[level, 2 * i * width : (2 * i + 1) * width] = terms[i]
                b_s[level, (2 * i + 1) * width : (2 * i + 2) * width] = folded[i]

    def take_y(off):
        block = col ^ off
        rows, cols = grid_of((depth, width), block * depth)
        lower = jnp.where(
            rows > cols,
            y_v[block],
            jnp.where(rows == cols, jnp.float32(1.0), jnp.float32(0.0)),
        )
        place = pl.ds(pl.multiple_of(block * depth, depth), depth)
        high, low = split(lower)
        yr_s[0, place, :] = high
        yr_s[1, place, :] = low
        across = stack(lower.T)
        for p in range(pairs):
            term = dot3(across, pair_of(p, place))
            p_v[p] = term if off == 0 else p_v[p] + term

    load_v.wait()
    load_tt.wait()
    load_t.wait()
    t_s[...] = stack(triangle_factor(t_v[...]).T)
    prepare(0)
    for k in range(chunks):
        load_c(k).wait()
    for p in range(pairs):
        top = pair_of(p, slice(0, width))
        ahead = jnp.where(leads(0), top, dot3(a_s[0], top))
        z_v[0, 2 * p] = ahead[:, :chunk]
        z_v[0, 2 * p + 1] = ahead[:, chunk:]
    take_y(0)
    order = sorted(range(1, n_col), key=lambda off: (bin(off).count("1"), off))
    for off in order:
        for part in range(parts):
            arrived_y(off, part).wait_recv()
            for bit in bits:
                if bit < off & -off:
                    send_y(off, bit, part).start()
        if off == order[0]:
            take_y(off)
            for level in range(1, levels):
                prepare(level)
        else:
            take_y(off)
    upper = jnp.concatenate([yr_s[0, :width, :], yr_s[1, :width, :]], axis=0)
    straight = upper[:width].astype(jnp.float32) + upper[width:].astype(jnp.float32)
    folded = split(jnp.where(leads(0), straight, dot3(a_s[0], straight)))
    for i in range(2):
        f_s[2 * i * width : (2 * i + 1) * width] = yr_s[i, :width, :]
        f_s[(2 * i + 1) * width : (2 * i + 2) * width] = folded[i]

    def exchange(level, k):
        return pltpu.make_async_remote_copy(
            src_ref=z_v.at[level, k],
            dst_ref=r_v.at[level, k],
            send_sem=s_sem.at[level, k],
            recv_sem=r_sem.at[level, k],
            device_id=(row ^ (1 << level), col),
            device_id_type=MESH,
        )

    def local(p):
        weight = dot3(t_s[...], p_v[p])
        w_v[p] = weight
        change = dot3(f_s[...], weight)
        for i in range(2):
            k = 2 * p + i
            side = slice(i * chunk, (i + 1) * chunk)
            z_v[0, k] = z_v[0, k] - change[width:, side]
            exchange(0, k).start()
            c_v[k, :width, :] = c_v[k, :width, :] - change[:width, side]

    def combine(level, k):
        top = c_v[k, :width, :]
        ahead = jnp.where(leads(level + 1), top, dot3(a_s[level + 1], top))
        exchange(level, k).wait_recv()
        change = dot3(b_s[level], z_v[level, k] + r_v[level, k])
        z_v[level + 1, k] = ahead - change[width:]
        exchange(level + 1, k).start()
        c_v[k, :width, :] = top - change[:width]

    def last(k):
        level = levels - 1
        exchange(level, k).wait_recv()
        lhs = jnp.concatenate([b_s[level, :width], b_s[level, 2 * width : 3 * width]], axis=0)
        c_v[k, :width, :] = c_v[k, :width, :] - dot3(lhs, z_v[level, k] + r_v[level, k])

    def store_top(k):
        return pltpu.make_async_copy(
            c_v.at[k, pl.ds(0, width), :], out_hbm.at[pl.ds(0, width), columns(k)], out_sem.at[0, k]
        )

    def store_rest(k):
        return pltpu.make_async_copy(
            c_v.at[k, pl.ds(width, rest), :],
            out_hbm.at[pl.ds(width, rest), columns(k)],
            out_sem.at[1, k],
        )

    local(0)

    def step(t, carry):
        @pl.when((lax.rem(t, 2) == 0) & (t // 2 + 1 < pairs))
        def _():
            local(t // 2 + 1)

        for level in range(levels - 1):
            k = t - level

            @pl.when((k >= 0) & (k < chunks))
            def _():
                combine(level, k)

        return carry

    lax.fori_loop(0, chunks + levels - 2, step, 0)

    def finish(p, carry):
        lhs = jnp.concatenate([yr_s[0, width:, :], yr_s[1, width:, :]], axis=0)
        change = dot3(lhs, w_v[p])
        for i in range(2):
            k = 2 * p + i
            c_v[k, width:, :] = c_v[k, width:, :] - change[:, i * chunk : (i + 1) * chunk]
            store_rest(k).start()
        for i in range(2):
            last(2 * p + i)
            store_top(2 * p + i).start()
        return carry

    lax.fori_loop(0, pairs, finish, 0)

    for bit in bits:
        for off in range(0, n_col, 2 * bit):
            for part in range(parts):
                send_y(off, bit, part).wait_send()

    def drain(k, carry):
        for level in range(levels):
            exchange(level, k).wait_send()
        store_top(k).wait()
        store_rest(k).wait()
        return carry

    lax.fori_loop(0, chunks, drain, 0)


def per_device(trailing, panel_y, panel_t, tree_v, tree_t):
    n_col = lax.axis_size("col")
    depth, width = panel_y.shape
    height, extent = trailing.shape
    levels = tree_v.shape[0]
    chunk = min(CHUNK, extent)
    chunks = extent // chunk
    f32, bf16 = jnp.float32, jnp.bfloat16
    products = height * width * 2 + width * width * (1 + 2 * levels)
    return pl.pallas_call(
        functools.partial(kernel, n_col, levels, chunks, width, depth, PARTS),
        out_shape=pltpu.VMEM(trailing.shape, f32),
        in_specs=[pl.BlockSpec(memory_space=pltpu.HBM)] * 5,
        out_specs=pl.BlockSpec(memory_space=pl.ANY),
        scratch_shapes=[
            pltpu.VMEM((chunks, height, chunk), f32),
            pltpu.VMEM((n_col, depth, width), f32),
            pltpu.VMEM((width, width), f32),
            pltpu.VMEM((levels, width, width), f32),
            pltpu.VMEM((levels, width, width), f32),
            pltpu.VMEM((chunks // 2, width, 2 * chunk), f32),
            pltpu.VMEM((chunks // 2, width, 2 * chunk), f32),
            pltpu.VMEM((levels, chunks, width, chunk), f32),
            pltpu.VMEM((levels, chunks, width, chunk), f32),
            pltpu.VMEM((2, height, width), bf16),
            pltpu.VMEM((2 * width, width), bf16),
            pltpu.VMEM((levels, 2 * width, width), bf16),
            pltpu.VMEM((levels, 4 * width, width), bf16),
            pltpu.VMEM((4 * width, width), bf16),
            pltpu.SemaphoreType.DMA((chunks,)),
            pltpu.SemaphoreType.DMA((4,)),
            pltpu.SemaphoreType.DMA((2, chunks)),
            pltpu.SemaphoreType.DMA((PARTS, n_col)),
            pltpu.SemaphoreType.DMA((PARTS, n_col)),
            pltpu.SemaphoreType.DMA((levels, chunks)),
            pltpu.SemaphoreType.DMA((levels, chunks)),
        ],
        compiler_params=pltpu.CompilerParams(
            collective_id=0, has_side_effects=True, vmem_limit_bytes=56 * 1024 * 1024
        ),
        cost_estimate=pl.CostEstimate(
            flops=6 * products * extent,
            bytes_accessed=8 * height * extent,
            transcendentals=0,
        ),
    )(trailing, panel_y, panel_t, tree_v, tree_t)


def solution(mesh):
    placed = (
        P("row", "col"),
        P(("row", "col"), None),
        P("row", None),
        P(None, "row", None),
        P(None, "row", None),
    )
    return jax.shard_map(
        per_device, mesh=mesh, in_specs=placed, out_specs=P("row", "col"), check_vma=False
    )
```

time: 82.8 us -> 76.2 us (0.920)
  local copies, waits for them, and re-layouts: 8.37 us -> 2.02 us
    unnamed x11 -> x1, local copies, waits for them, and re-layouts: 8.37 us -> 2.02 us
where the time goes in v2:
time: 76.2 us; the launch traced here: 76.1 us
  Pallas kernels  74 us (97%)
  local copies, waits for them, and re-layouts  2.02 us (3%)
    pallas_call x1, Pallas kernels, per_device(): pl.pallas_call(functools.partial(kernel, n_col, levels, chunks, width, de...  74 us
    unnamed x1, local copies, waits for them, and re-layouts  2.02 us

profile of v2, /device:TPU:0, one launch (start us, length us, event | category | flops | bytes accessed | tf_op | source)
XLA Modules:
  0.0 76.1 jit_solution(5683095647100967519)
XLA Ops:
  0.0 74.0 %shard_map.55 = f32[1024,1024]{1,0:T(8,128)S(1)} custom-call(f32[1024,1024]{1,0:T(8,128)} %c_hbm.1, f32[256,256]{1,0:T(8,128)} %y_hbm.1, f32[256,256]{1,0:T(8,128)} %t_hbm.1, f32[3,256,256]{2,1,0:T(8,128)} %v_hbm.1, f32[3,256,256]{2,1,0:T(8,128)} %tt_hbm.1), custom_call_target="tpu_custom_call" | custom-call | flops 6039797760 | bytes 8388608 | tf_op jit(solution)/shard_map/pallas_call | solution.py:292
  74.0 2.0 %copy.7 = f32[1024,1024]{1,0:T(8,128)} copy(f32[1024,1024]{1,0:T(8,128)S(1)} %shard_map.55) | data formatting | bytes 8388608

commit v3 on v2

--- a/solution.py
+++ b/solution.py
@@ -50,7 +50,7 @@
     n_col, levels, chunks, width, depth, parts,
     c_hbm, y_hbm, t_hbm, v_hbm, tt_hbm, out_hbm,
     c_v, y_v, t_v, v_v, tt_v, p_v, w_v, z_v, r_v,
-    yr_s, t_s, a_s, b_s, f_s,
+    yr_s, yt_s, t_s, a_s, b_s, f_s,
     c_sem, in_sem, out_sem, ys_sem, yr_sem, s_sem, r_sem,
 ):
     row = lax.axis_index("row")
@@ -83,13 +83,12 @@
     load_t.start()
     for k in range(chunks):
         load_c(k).start()
-    own_y.wait()
     pl.semaphore_wait(barrier, len(partners))
 
     def send_y(off, bit, part):
         place = y_v.at[col ^ off, pl.ds(part * share, share), :]
         return pltpu.make_async_remote_copy(
-            src_ref=place,
+            src_ref=y_hbm.at[pl.ds(part * share, share), :] if off == 0 else place,
             dst_ref=place,
             send_sem=ys_sem.at[part, off | bit],
             recv_sem=yr_sem.at[part, off | bit],
@@ -147,10 +146,12 @@
         high, low = split(lower)
         yr_s[0, place, :] = high
         yr_s[1, place, :] = low
-        across = stack(lower.T)
-        for p in range(pairs):
-            term = dot3(across, pair_of(p, place))
-            p_v[p] = term if off == 0 else p_v[p] + term
+        yt_s[off] = stack(lower.T)
+
+    def product(off, p):
+        block = col ^ off
+        place = pl.ds(pl.multiple_of(block * depth, depth), depth)
+        return dot3(yt_s[off], pair_of(p, place))
 
     load_v.wait()
     load_tt.wait()
@@ -164,20 +165,30 @@
         ahead = jnp.where(leads(0), top, dot3(a_s[0], top))
         z_v[0, 2 * p] = ahead[:, :chunk]
         z_v[0, 2 * p + 1] = ahead[:, chunk:]
+    own_y.wait()
     take_y(0)
     order = sorted(range(1, n_col), key=lambda off: (bin(off).count("1"), off))
-    for off in order:
+    late = order[1:]
+
+    def arrive(off):
         for part in range(parts):
             arrived_y(off, part).wait_recv()
             for bit in bits:
                 if bit < off & -off:
                     send_y(off, bit, part).start()
-        if off == order[0]:
-            take_y(off)
-            for level in range(1, levels):
-                prepare(level)
-        else:
-            take_y(off)
+
+    for p in range(pairs):
+        p_v[p] = product(0, p)
+    for off in order[:1]:
+        arrive(off)
+        take_y(off)
+        for p in range(pairs):
+            p_v[p] = p_v[p] + product(off, p)
+    for level in range(1, levels):
+        prepare(level)
+    for off in late:
+        arrive(off)
+        take_y(off)
     upper = jnp.concatenate([yr_s[0, :width, :], yr_s[1, :width, :]], axis=0)
     straight = upper[:width].astype(jnp.float32) + upper[width:].astype(jnp.float32)
     folded = split(jnp.where(leads(0), straight, dot3(a_s[0], straight)))
@@ -196,20 +207,32 @@
         )
 
     def local(p):
-        weight = dot3(t_s[...], p_v[p])
+        proj = p_v[p]
+        for off in late:
+            proj = proj + product(off, p)
+        weight = dot3(t_s[...], proj)
         w_v[p] = weight
         change = dot3(f_s[...], weight)
         for i in range(2):
             k = 2 * p + i
             side = slice(i * chunk, (i + 1) * chunk)
             z_v[0, k] = z_v[0, k] - change[width:, side]
-            exchange(0, k).start()
+            if i == 0:
+                @pl.when(p == 0)
+                def _():
+                    exchange(0, k).start()
             c_v[k, :width, :] = c_v[k, :width, :] - change[:width, side]
 
     def combine(level, k):
         top = c_v[k, :width, :]
         ahead = jnp.where(leads(level + 1), top, dot3(a_s[level + 1], top))
         exchange(level, k).wait_recv()
+        if level == 0:
+
+            @pl.when(k + 1 < chunks)
+            def _():
+                exchange(0, k + 1).start()
+
         change = dot3(b_s[level], z_v[level, k] + r_v[level, k])
         z_v[level + 1, k] = ahead - change[width:]
         exchange(level + 1, k).start()
@@ -241,15 +264,15 @@
             local(t // 2 + 1)
 
         for level in range(levels - 1):
-            k = t - level
-
-            @pl.when((k >= 0) & (k < chunks))
+            k = jnp.where(t == 2 * level - 1, 0, t - 2 * level)
+
+            @pl.when((k >= min(level, 1)) & (k < chunks) | (t == 2 * level - 1))
             def _():
                 combine(level, k)
 
         return carry
 
-    lax.fori_loop(0, chunks + levels - 2, step, 0)
+    lax.fori_loop(0, chunks + 2 * (levels - 2), step, 0)
 
     def finish(p, carry):
         lhs = jnp.concatenate([yr_s[0, width:, :], yr_s[1, width:, :]], axis=0)
@@ -305,6 +328,7 @@
             pltpu.VMEM((levels, chunks, width, chunk), f32),
             pltpu.VMEM((levels, chunks, width, chunk), f32),
             pltpu.VMEM((2, height, width), bf16),
+            pltpu.VMEM((n_col, 2 * width, depth), bf16),
             pltpu.VMEM((2 * width, width), bf16),
             pltpu.VMEM((levels, 2 * width, width), bf16),
             pltpu.VMEM((levels, 4 * width, width), bf16),

time: 76.2 us -> 77.4 us (1.016)
  Pallas kernels: 74 us -> 75.2 us
    pallas_call x1, Pallas kernels: 74 us -> 75.2 us  [per_device(): pl.pallas_call(functools.partial(kernel, n_col, levels, chunks, width, de...]
where the time goes in v3:
time: 77.4 us; the launch traced here: 77.3 us
  Pallas kernels  75.2 us (97%)
  local copies, waits for them, and re-layouts  2.02 us (3%)
    pallas_call x1, Pallas kernels, per_device(): pl.pallas_call(functools.partial(kernel, n_col, levels, chunks, width, de...  75.2 us
    unnamed x1, local copies, waits for them, and re-layouts  2.02 us

profile of v3, /device:TPU:0, one launch (start us, length us, event | category | flops | bytes accessed | tf_op | source)
XLA Modules:
  0.0 77.3 jit_solution(7659788929953530179)
XLA Ops:
  0.0 75.2 %shard_map.55 = f32[1024,1024]{1,0:T(8,128)S(1)} custom-call(f32[1024,1024]{1,0:T(8,128)} %c_hbm.1, f32[256,256]{1,0:T(8,128)} %y_hbm.1, f32[256,256]{1,0:T(8,128)} %t_hbm.1, f32[3,256,256]{2,1,0:T(8,128)} %v_hbm.1, f32[3,256,256]{2,1,0:T(8,128)} %tt_hbm.1), custom_call_target="tpu_custom_call" | custom-call | flops 6039797760 | bytes 8388608 | tf_op jit(solution)/shard_map/pallas_call | solution.py:315
  75.2 2.0 %copy.7 = f32[1024,1024]{1,0:T(8,128)} copy(f32[1024,1024]{1,0:T(8,128)S(1)} %shard_map.55) | data formatting | bytes 8388608
